TPU v7x, 32 devices: a whole 2x2x4 slice. The times are simulated.
32 devices in a mesh: dp: 16 (over z, y, core), tensor: 2 (over x).
Axes of the slice: x: 2, y: 2, z: 4, core: 2. Of those that a mesh axis runs over, the one named last changes fastest.
Arguments:
- tokens: bfloat16 [6144, 4096], P(('dp', 'tensor')), may hold values from -21 to 21
- wq_codes: bfloat16 [4096, 1024], P('dp', 'tensor'), may hold values from -4 to 4
- wq_scales: float32 [32, 8], replicated, may hold values from 0.0078125 to 0.03125
- wk_codes: bfloat16 [4096, 128], P('dp', 'tensor'), may hold values from -4 to 4
- wk_scales: float32 [32, 1], replicated, may hold values from 0.0078125 to 0.03125
- wv_codes: bfloat16 [4096, 128], P('dp', 'tensor'), may hold values from -4 to 4
- wv_scales: float32 [32, 1], replicated, may hold values from 0.0078125 to 0.03125
- wo_codes: bfloat16 [1024, 4096], P('tensor', 'dp'), may hold values from -4 to 4
- wo_scales: float32 [8, 32], replicated, may hold values from 0.015625 to 0.0625
Outputs:
- mixed: bfloat16 [6144, 4096], P(('dp', 'tensor'))
All inputs are finite; a program needn't handle non-finite values.
Results may differ from a plain program's by a relative error of at most 0.014.
The roundings to bfloat16 on the way count: a program that leaves them out, or rounds other values in their place, can miss the bound.
Values may be sent and summed in bfloat16 or wider, within the bound.
A program may use at most 64 MiB of HBM per device.

v0:
```python
import jax
import jax.numpy as jnp
from jax import lax
from jax.sharding import PartitionSpec as P

HEAD = 128
BLOCK = 128
SPAN = 384
rope_base = 500000.0
masked_value = -1e30


def from_partner(value, axis, apart):
    mask = 2**apart
    pairs = [(source, source ^ mask) for source in range(lax.axis_size(axis))]
    return lax.ppermute(value, axis, pairs)


def dequantize(codes, scales, row_start, col_start):
    height, breadth = codes.shape
    row_block = (row_start + jnp.arange(height, dtype=jnp.int32)) // BLOCK
    col_block = (col_start + jnp.arange(breadth, dtype=jnp.int32)) // BLOCK
    row_pick = (row_block[:, None] == jnp.arange(scales.shape[0], dtype=jnp.int32)[None, :]).astype(
        jnp.float32
    )
    col_pick = (col_block[None, :] == jnp.arange(scales.shape[1], dtype=jnp.int32)[:, None]).astype(
        jnp.float32
    )
    picked = jnp.dot(row_pick, scales, precision=lax.Precision.HIGHEST)
    expanded = jnp.dot(picked, col_pick, precision=lax.Precision.HIGHEST)
    return (codes.astype(jnp.float32) * expanded).astype(jnp.bfloat16)


def rotate(features, positions):
    half_size = HEAD // 2
    steps = jnp.arange(half_size).astype(jnp.float32)
    inverse = jnp.exp(-(2.0 * steps / HEAD) * jnp.log(jnp.float32(rope_base)))
    angle = positions[:, None] * inverse[None, :]
    cosine = jnp.cos(angle)[:, None, :]
    sine = jnp.sin(angle)[:, None, :]
    first = features[..., :half_size]
    second = features[..., half_size:]
    return jnp.concatenate(
        [first * cosine - second * sine, second * cosine + first * sine], axis=-1
    )


def in_order(upper, mine, partner):
    return jnp.where(
        upper, jnp.concatenate([partner, mine], axis=1), jnp.concatenate([mine, partner], axis=1)
    )


def body(
    tokens, wq_codes, wq_scales, wk_codes, wk_scales, wv_codes, wv_scales, wo_codes, wo_scales
):
    data_index = lax.axis_index("dp")
    head_index = lax.axis_index("tensor")
    weight_rows = wq_codes.shape[0]
    row_start = data_index * weight_rows
    query_width = wq_codes.shape[1]
    shard_width = wk_codes.shape[1]
    wq_local = dequantize(wq_codes, wq_scales, row_start, head_index * query_width)
    wk_local = dequantize(wk_codes, wk_scales, row_start, head_index * shard_width)
    wv_local = dequantize(wv_codes, wv_scales, row_start, head_index * shard_width)
    wo_local = dequantize(
        wo_codes, wo_scales, head_index * wo_codes.shape[0], data_index * wo_codes.shape[1]
    )
    wo_whole = lax.all_gather(wo_local, "dp", axis=1, tiled=True)
    sequence = lax.all_gather(tokens, "tensor", axis=0, tiled=True)
    upper = head_index % 2 == 1
    partner_k, partner_v = from_partner((wk_local, wv_local), "tensor", 0)
    wk_used = in_order(upper, wk_local, partner_k)
    wv_used = in_order(upper, wv_local, partner_v)
    length = sequence.shape[0]
    full_q, full_k, full_v = (
        lax.all_gather(wq_local, "dp", axis=0, tiled=True),
        lax.all_gather(wk_used, "dp", axis=0, tiled=True),
        lax.all_gather(wv_used, "dp", axis=0, tiled=True),
    )
    query_lin = jnp.dot(sequence, full_q, preferred_element_type=jnp.float32)
    key_lin = jnp.dot(sequence, full_k, preferred_element_type=jnp.float32)
    value_lin = jnp.dot(sequence, full_v, preferred_element_type=jnp.float32)
    positions = (jnp.arange(length) % SPAN).astype(jnp.float32)
    heads_here = query_width // HEAD
    span_count = length // SPAN
    queries = rotate(query_lin.reshape(length, heads_here, HEAD), positions).astype(jnp.bfloat16)
    keys = rotate(key_lin.reshape(length, 1, HEAD), positions)[:, 0, :].astype(jnp.bfloat16)
    values = value_lin.astype(jnp.bfloat16)
    queries = queries.reshape(span_count, SPAN, heads_here, HEAD)
    keys = keys.reshape(span_count, SPAN, HEAD)
    values = values.reshape(span_count, SPAN, HEAD)
    causal = jnp.arange(SPAN)[:, None] >= jnp.arange(SPAN)[None, :]
    scores = jnp.einsum("cqhd,ckd->chqk", queries, keys, preferred_element_type=jnp.float32) * (
        1.0 / HEAD**0.5
    )
    scores = jnp.where(causal[None, None, :, :], scores, masked_value)
    peak = jnp.max(scores, axis=-1, keepdims=True)
    powers = jnp.exp(scores - peak)
    total = jnp.sum(powers, axis=-1, keepdims=True)
    probs = (powers / total).astype(jnp.bfloat16)
    attended = (
        jnp.einsum("chqk,ckd->cqhd", probs, values, preferred_element_type=jnp.float32)
        .astype(jnp.bfloat16)
        .reshape(length, query_width)
    )
    terms = jnp.dot(attended, wo_whole, preferred_element_type=jnp.float32)
    mixed = lax.psum_scatter(terms.astype(jnp.bfloat16), "tensor", scatter_dimension=0, tiled=True)
    return mixed


def solution(mesh):
    return jax.shard_map(
        body,
        mesh=mesh,
        in_specs=(
            P(("dp", "tensor"), None),
            P("dp", "tensor"),
            P(),
            P("dp", "tensor"),
            P(),
            P("dp", "tensor"),
            P(),
            P("tensor", "dp"),
            P(),
        ),
        out_specs=P(("dp", "tensor"), None),
        check_vma=False,
    )
```

profile of v0, /device:TPU:0, one launch (start us, length us, event | category | flops | bytes accessed | tf_op | source)
XLA Modules:
  0.0 298.7 jit_solution(14492165854905876810)
XLA Ops:
  6.5 0.0 copy-start
  6.5 0.0 copy-start.3
  6.5 0.0 copy-start.4
  6.5 0.0 all-gather.10.cloned.1.call-start
  6.6 0.9 fusion.18
  7.5 0.9 fusion.17
  8.4 0.9 multiply_convert_fusion.1
  9.3 3.0 %collective-permute-start.1 = (bf16[256,64]{0,1:T(8,128)(2,1)S(1)}, bf16[256,64]{0,1:T(8,128)(2,1)S(1)}, u32[]{:S(2)}, u32[]{:S(2)}) collective-permute-start(bf16[256,64]{0,1:T(8,128)(2,1)S(1)} %get-tuple-element.14), channel_id=1, source_target_pairs={{0,1},{1,0},{2,3},{3,2},{4,5},{5,4},{6,7},{7,6},{8,9},{9,8},{10,11... | collective-permute-start | bytes 98312 | tf_op jit(solution)/shard_map/ppermute | solution.py:16
  12.3 1.9 collective-permute-done.1
  14.2 0.6 maximum_select_fusion.1
  14.9 0.0 all-gather.10.cloned.1.call-update
  14.9 0.0 all-gather.8.cloned.1.call-start
  14.9 0.7 all-gather.8.cloned.1.call-update
  15.6 0.0 all-gather.12.cloned.1.call-start
  15.7 0.9 fusion.16
  16.7 0.0 copy-done.3
  16.7 1.1 fusion.2
  17.7 0.0 all-gather.12.cloned.1.call-update
  17.8 0.0 all-gather.6.cloned.1.call-start
  17.8 2.1 collective-permute-start
  19.9 1.9 collective-permute-done
  21.8 0.6 maximum_select_fusion
  22.4 0.0 all-gather.6.cloned.1.call-update
  22.4 0.0 all-gather.14.cloned.1.call-start
  22.5 0.0 copy-done
  22.5 0.3 fusion.10
  22.8 0.0 copy-done.4
  22.8 1.1 fusion.3
  23.9 0.0 all-gather.14.cloned.1.call-update
  23.9 0.0 reduce-scatter.2.cloned.1.call-start
  24.1 1.4 multiply_cosine_fusion
  25.5 28.1 %all-gather.10.cloned.1.call-done = bf16[4096,128]{0,1:T(8,128)(2,1)} async-done(((bf16[256,128]{0,1:T(8,128)(2,1)}), bf16[4096,128]{0,1:T(8,128)(2,1)}) %all-gather.10.cloned.1.call-update) | async-done | bytes 1048592 | tf_op jit(solution)/shard_map/all_gather | solution.py:78
  53.6 46.0 %all-gather.8.cloned.1.call-done = bf16[384,4096]{1,0:T(8,128)(2,1)} async-done(((bf16[192,4096]{1,0:T(8,128)(2,1)}), bf16[384,4096]{1,0:T(8,128)(2,1)}) %all-gather.8.cloned.1.call-update) | async-done | bytes 3145744 | tf_op jit(solution)/shard_map/all_gather | solution.py:70
  99.6 0.0 copy-start.1
  99.6 3.4 %convolution_bitcast_fusion = f32[384,1,128]{0,2,1:T(8,128)S(1)} fusion(bf16[4096,128]{0,1:T(8,128)(2,1)} %all-gather.10.cloned.1.call-done, bf16[384,4096]{1,0:T(8,128)(2,1)} %all-gather.8.cloned.1.call-done), kind=kOutput, calls=%fused_computation.12 | convolution fusion | flops 402653184 | bytes 4390912 | tf_op jit(solution)/shard_map/dot_general | solution.py:82
  103.1 1.1 fusion.20
  104.1 48.3 %all-gather.12.cloned.1.call-done = bf16[4096,512]{1,0:T(8,128)(2,1)} async-done(((bf16[256,512]{1,0:T(8,128)(2,1)}), bf16[4096,512]{1,0:T(8,128)(2,1)}) %all-gather.12.cloned.1.call-update) | async-done | bytes 4194320 | tf_op jit(solution)/shard_map/all_gather | solution.py:77
  152.4 0.0 copy-done.1
  152.4 4.6 %fusion.37 = f32[512,384]{1,0:T(8,128)S(1)} fusion(bf16[4096,512]{1,0:T(8,128)(2,1)} %all-gather.12.cloned.1.call-done, bf16[384,4096]{1,0:T(8,128)(2,1)S(1)} %copy-done.1), kind=kOutput, calls=%fused_computation.79 | convolution fusion | flops 1610612736 | bytes 8126464 | tf_op jit(solution)/shard_map/dot_general | solution.py:81
  157.0 0.0 copy-start.2
  157.0 0.1 fusion.36
  157.1 0.0 copy-start.5
  157.1 0.3 copy.17
  157.4 0.3 copy.18
  157.6 0.3 copy-done.2
  157.9 0.2 subtract_convert_fusion
  158.1 0.0 copy-done.5
  158.2 0.7 fusion.1
  158.9 0.5 fusion
  159.4 30.4 %all-gather.6.cloned.1.call-done = bf16[4096,128]{0,1:T(8,128)(2,1)} async-done(((bf16[256,128]{0,1:T(8,128)(2,1)}), bf16[4096,128]{0,1:T(8,128)(2,1)}) %all-gather.6.cloned.1.call-update) | async-done | bytes 1048592 | tf_op jit(solution)/shard_map/all_gather | solution.py:79
  189.7 4.1 %convolution_convert_fusion.1 = bf16[128,4,384]{2,0,1:T(8,128)(2,1)S(1)} fusion(f32[384,384,4]{1,0,2:T(8,128)S(1)} %get-tuple-element.16, f32[4,384]{1,0:T(4,128)S(1)} %fusion, f32[4,384]{1,0:T(4,128)S(1)} %get-tuple-element.15, pred[384,384]{0,1:T(8,128)(4,1)S(1)} %iota_compare_fusion, bf16[4096,128]{0,1:T(8,128)(2,1)} %all-gather.6.cloned.1.call-done, ...), kind=kOutput, calls=%fused_computation.6 | convolution fusion | flops 556843008 | bytes 7106560 | tf_op jit(solution)/shard_map/chqk,ckd->cqhd/dot_general | solution.py:103
  193.8 50.7 %all-gather.14.cloned.1.call-done = bf16[512,4096]{1,0:T(8,128)(2,1)} async-done(((bf16[512,256]{1,0:T(8,128)(2,1)}), bf16[512,4096]{1,0:T(8,128)(2,1)}) %all-gather.14.cloned.1.call-update) | async-done | bytes 4194320 | tf_op jit(solution)/shard_map/all_gather | solution.py:69
  244.5 5.7 %convolution_convert_fusion = bf16[384,4096]{1,0:T(8,128)(2,1)} fusion(bf16[384,512]{0,1:T(8,128)(2,1)S(1)} %bitcast.58, bf16[512,4096]{1,0:T(8,128)(2,1)} %all-gather.14.cloned.1.call-done), kind=kOutput, calls=%fused_computation | convolution fusion | flops 1612185600 | bytes 7733248 | tf_op jit(solution)/shard_map/dot_general | solution.py:107
  250.2 0.0 reduce-scatter.2.cloned.1.call-update
  250.2 41.7 %reduce-scatter.2.cloned.1.call-done = bf16[192,4096]{1,0:T(8,128)(2,1)} async-done(((bf16[384,4096]{1,0:T(8,128)(2,1)}), bf16[192,4096]{1,0:T(8,128)(2,1)}) %reduce-scatter.2.cloned.1.call-update) | async-done | bytes 1572880 | tf_op jit(solution)/shard_map/reduce_scatter | solution.py:108
  (6 shorter events, 0.1 us)
Async XLA Ops:
  6.5 16.0 %copy-start = (f32[8,32]{1,0:T(8,128)S(1)}, f32[8,32]{1,0:T(8,128)}, u32[]{:S(2)}) copy-start(f32[8,32]{1,0:T(8,128)} %param.17) | copy-start | bytes 3076
  6.5 10.1 %copy-start.3 = (bf16[256,512]{1,0:T(8,128)(2,1)S(1)}, bf16[256,512]{1,0:T(8,128)(2,1)}, u32[]{:S(2)}) copy-start(bf16[256,512]{1,0:T(8,128)(2,1)} %param.10) | copy-start | bytes 786436
  6.5 16.3 %copy-start.4 = (bf16[512,256]{1,0:T(8,128)(2,1)S(1)}, bf16[512,256]{1,0:T(8,128)(2,1)}, u32[]{:S(2)}) copy-start(bf16[512,256]{1,0:T(8,128)(2,1)} %param.16) | copy-start | bytes 786436
  6.5 47.1 %all-gather.10.cloned.1.call-start = ((), (), s32[]{:S(2)}) async-start(), calls=%async_computation.3 | async-start | bytes 1114112 | tf_op jit(solution)/shard_map/all_gather | solution.py:78
  9.3 4.9 %collective-permute-start.1 = (bf16[256,64]{0,1:T(8,128)(2,1)S(1)}, bf16[256,64]{0,1:T(8,128)(2,1)S(1)}, u32[]{:S(2)}, u32[]{:S(2)}) collective-permute-start(bf16[256,64]{0,1:T(8,128)(2,1)S(1)} %get-tuple-element.14), channel_id=1, source_target_pairs={{0,1},{1,0},{2,3},{3,2},{4,5},{5,4},{6,7},{7,6},{8,9},{9,8},{10,11... | collective-permute-start | bytes 98312 | tf_op jit(solution)/shard_map/ppermute | solution.py:16
  14.9 84.7 %all-gather.8.cloned.1.call-start = ((), (), s32[]{:S(2)}) async-start(), calls=%async_computation.2 | async-start | bytes 4718592 | tf_op jit(solution)/shard_map/all_gather | solution.py:70
  15.6 136.8 %all-gather.12.cloned.1.call-start = ((), (), s32[]{:S(2)}) async-start(), calls=%async_computation.4 | async-start | bytes 4456448 | tf_op jit(solution)/shard_map/all_gather | solution.py:77
  17.8 172.0 %all-gather.6.cloned.1.call-start = ((), (), s32[]{:S(2)}) async-start(), calls=%async_computation.1 | async-start | bytes 1114112 | tf_op jit(solution)/shard_map/all_gather | solution.py:79
  17.8 4.0 %collective-permute-start = (bf16[256,64]{0,1:T(8,128)(2,1)S(1)}, bf16[256,64]{0,1:T(8,128)(2,1)S(1)}, u32[]{:S(2)}, u32[]{:S(2)}) collective-permute-start(bf16[256,64]{0,1:T(8,128)(2,1)S(1)} %get-tuple-element.13), channel_id=1, source_target_pairs={{0,1},{1,0},{2,3},{3,2},{4,5},{5,4},{6,7},{7,6},{8,9},{9,8},{10,11... | collective-permute-start | bytes 98312 | tf_op jit(solution)/shard_map/ppermute | solution.py:16
  22.4 222.0 %all-gather.14.cloned.1.call-start = ((), (), s32[]{:S(2)}) async-start(), calls=%async_computation.5 | async-start | bytes 4456448 | tf_op jit(solution)/shard_map/all_gather | solution.py:69
  23.9 267.9 %reduce-scatter.2.cloned.1.call-start = ((), (), s32[]{:S(2)}) async-start(), calls=%async_computation.6 | async-start | bytes 4718592 | tf_op jit(solution)/shard_map/reduce_scatter | solution.py:108
  99.6 52.8 %copy-start.1 = (bf16[384,4096]{1,0:T(8,128)(2,1)S(1)}, bf16[384,4096]{1,0:T(8,128)(2,1)}, u32[]{:S(2)}) copy-start(bf16[384,4096]{1,0:T(8,128)(2,1)} %all-gather.8.cloned.1.call-done) | copy-start | bytes 9437188
  157.0 0.9 copy-start.2
  157.1 1.1 copy-start.5
Sparse Core Ops, SparseCore 0:
  15.0 38.5 all-gather.9
  55.2 44.4 all-gather.7
  101.8 50.5 all-gather.11
  154.4 35.2 all-gather.5
  191.7 52.6 all-gather.13
  250.3 41.4 reduce-scatter.1
where the time goes:
time: 299 us
  waiting for transfers between devices  250 us (84%)
  matrix products  23.7 us (8%)
  between operations  13.7 us (5%)
  other arithmetic  5.51 us (2%)
  starting transfers between devices  5.3 us (2%)
    all_gather x1, waiting for transfers between devices, body(): wo_whole = lax.all_gather(wo_local, 'dp', axis=1, tiled=True)  50.7 us
    all_gather x1, waiting for transfers between devices, body(): lax.all_gather(wq_local, 'dp', axis=0, tiled=True)  48.3 us
    all_gather x1, waiting for transfers between devices, body(): sequence = lax.all_gather(tokens, 'tensor', axis=0, tiled=True)  46 us
    reduce_scatter x1, waiting for transfers between devices, body(): lax.psum_scatter(terms.astype(jnp.bfloat16), 'tensor', scatter_dimension=...  41.7 us
    all_gather x1, waiting for transfers between devices, body(): lax.all_gather(wv_used, 'dp', axis=0, tiled=True)  30.4 us
    all_gather x1, waiting for transfers between devices, body(): lax.all_gather(wk_used, 'dp', axis=0, tiled=True)  28.1 us
  transfers between devices with their start and end apart: 8, of which 8 were waited for; matrix products, arithmetic and copies ran while one was open for 7% of the time, Pallas kernels for 0%

commit v1 on v0

--- a/solution.py
+++ b/solution.py
@@ -8,6 +8,28 @@
 SPAN = 384
 rope_base = 500000.0
 masked_value = -1e30
+
+
+def in_order_2(tiles, dim):
+    tiles = jnp.moveaxis(tiles, 0, dim)
+    shape = tiles.shape
+    return tiles.reshape(*shape[:dim], shape[dim] * shape[dim + 1], *shape[dim + 2 :])
+
+
+def ring_gather(value, axis, dim):
+    length = lax.axis_size(axis)
+    pairs = [(i, (i + 1) % length) for i in range(length)]
+    back = [(b, a) for a, b in pairs]
+    lower, upper = ([], [])
+    for hop in range(length - 1):
+        if hop % 2 == 0:
+            lower.append(lax.ppermute(lower[-1] if lower else value, axis, pairs))
+        else:
+            upper.append(lax.ppermute(upper[-1] if upper else value, axis, back))
+    tiles = jnp.stack([*lower[::-1], value, *upper])
+    shift = lax.axis_index(axis) - len(lower)
+    tiles = tiles[(jnp.arange(length) - shift) % length]
+    return in_order_2(tiles, dim)
 
 
 def from_partner(value, axis, apart):
@@ -75,7 +97,7 @@
     length = sequence.shape[0]
     full_q, full_k, full_v = (
         lax.all_gather(wq_local, "dp", axis=0, tiled=True),
-        lax.all_gather(wk_used, "dp", axis=0, tiled=True),
+        ring_gather(wk_used, "dp", 0),
         lax.all_gather(wv_used, "dp", axis=0, tiled=True),
     )
     query_lin = jnp.dot(sequence, full_q, preferred_element_type=jnp.float32)

time: 299 us -> 258 us (0.86)
  waiting for transfers between devices: 250 us -> 179 us
  starting transfers between devices: 5.3 us -> 36.8 us
    all_gather x1, waiting for transfers between devices: 46 us -> 0.02 us  [body(): sequence = lax.all_gather(tokens, 'tensor', axis=0, tiled=True)]
    ppermute x0 -> x15, starting transfers between devices: none -> 31.5 us  [the longest x7 31.4 us: ring_gather(): upper.append(lax.ppermute(upper[-1] if upper else value, axis, back))]
    all_gather x1 -> x0, waiting for transfers between devices: 28.1 us -> none  [body(): lax.all_gather(wk_used, 'dp', axis=0, tiled=True)]
    ppermute x0 -> x15, waiting for transfers between devices: none -> 21.8 us  [the longest x8 17.8 us: ring_gather(): lower.append(lax.ppermute(lower[-1] if lower else value, axis, pairs))]
    all_gather x1, waiting for transfers between devices: 48.3 us -> 27.4 us  [body(): lax.all_gather(wq_local, 'dp', axis=0, tiled=True)]
  transfers between devices with their start and end apart: 8 -> 22, of which waited for: 8 -> 18; matrix products, arithmetic and copies ran while one was open for 7% -> 9% of each run, Pallas kernels for 0% -> 0%
where the time goes in v1:
time: 258 us
  waiting for transfers between devices  179 us (69%)
  starting transfers between devices  36.8 us (14%)
  matrix products  23.9 us (9%)
  between operations  13.4 us (5%)
  other arithmetic  3.26 us (1%)
    all_gather x1, waiting for transfers between devices, body(): wo_whole = lax.all_gather(wo_local, 'dp', axis=1, tiled=True)  50.1 us
    reduce_scatter x1, waiting for transfers between devices, body(): lax.psum_scatter(terms.astype(jnp.bfloat16), 'tensor', scatter_dimension=...  41.7 us
    ppermute x7, starting transfers between devices, ring_gather(): upper.append(lax.ppermute(upper[-1] if upper else value, axis, back))  31.4 us
    all_gather x1, waiting for transfers between devices, body(): lax.all_gather(wv_used, 'dp', axis=0, tiled=True)  31 us
    all_gather x1, waiting for transfers between devices, body(): lax.all_gather(wq_local, 'dp', axis=0, tiled=True)  27.4 us
    ppermute x8, waiting for transfers between devices, ring_gather(): lower.append(lax.ppermute(lower[-1] if lower else value, axis, pairs))  17.8 us
    ppermute x2, waiting for transfers between devices, from_partner(): return lax.ppermute(value, axis, pairs)  5.81 us
    dot_general x1, matrix products, body(): terms = jnp.dot(attended, wo_whole, preferred_element_type=jnp.float32)  5.69 us
  transfers between devices with their start and end apart: 22, of which 18 were waited for; matrix products, arithmetic and copies ran while one was open for 9% of the time, Pallas kernels for 0%

profile of v1, /device:TPU:0, one launch (start us, length us, event | category | flops | bytes accessed | tf_op | source)
XLA Modules:
  0.0 257.7 jit_solution(8792375805459228327)
XLA Ops:
  6.6 0.0 all-gather.7.cloned.1.call-start
  6.6 0.7 all-gather.7.cloned.1.call-update
  7.3 0.0 all-gather.9.cloned.1.call-start
  7.4 0.9 fusion.16
  8.3 2.2 fusion.2
  10.4 0.0 all-gather.9.cloned.1.call-update
  10.4 0.0 all-gather.5.cloned.1.call-start
  10.5 0.1 copy.18
  10.6 0.1 copy.19
  10.8 0.2 fusion.18
  11.0 0.3 fusion.17
  11.2 0.2 multiply_convert_fusion.1
  11.4 3.0 %collective-permute-start = (bf16[256,64]{1,0:T(8,128)(2,1)S(1)}, bf16[256,64]{1,0:T(8,128)(2,1)S(1)}, u32[]{:S(2)}, u32[]{:S(2)}) collective-permute-start(bf16[256,64]{1,0:T(8,128)(2,1)S(1)} %get-tuple-element.13), channel_id=1, source_target_pairs={{0,1},{1,0},{2,3},{3,2},{4,5},{5,4},{6,7},{7,6},{8,9},{9,8},{10,11... | collective-permute-start | bytes 98312 | tf_op jit(solution)/shard_map/ppermute | solution.py:38
  14.4 2.2 collective-permute-done
  16.7 0.7 maximum_select_fusion
  17.4 0.0 all-gather.5.cloned.1.call-update
  17.4 0.0 all-gather.11.cloned.1.call-start
  17.5 0.3 fusion.10
  17.8 0.0 copy-done.1
  17.9 1.2 fusion.3
  19.1 0.0 reduce-scatter.2.cloned.1.call-start
  19.1 2.1 collective-permute-start.1
  21.2 3.6 %collective-permute-done.1 = bf16[256,64]{1,0:T(8,128)(2,1)S(1)} collective-permute-done((bf16[256,64]{1,0:T(8,128)(2,1)S(1)}, bf16[256,64]{1,0:T(8,128)(2,1)S(1)}, u32[]{:S(2)}, u32[]{:S(2)}) %collective-permute-start.1) | collective-permute-done | bytes 32800 | tf_op jit(solution)/shard_map/ppermute | solution.py:38
  24.8 0.1 maximum_select_fusion.1
  24.9 0.1 collective-permute-start.2
  24.9 6.4 %collective-permute-done.2 = bf16[256,128]{1,0:T(8,128)(2,1)S(1)} collective-permute-done((bf16[256,128]{1,0:T(8,128)(2,1)S(1)}, bf16[256,128]{1,0:T(8,128)(2,1)S(1)}, u32[]{:S(2)}, u32[]{:S(2)}) %collective-permute-start.2) | collective-permute-done | bytes 65568 | tf_op jit(solution)/shard_map/ppermute | solution.py:26
  31.3 4.4 %collective-permute-start.10 = (bf16[256,128]{1,0:T(8,128)(2,1)S(1)}, bf16[256,128]{1,0:T(8,128)(2,1)S(1)}, u32[]{:S(2)}, u32[]{:S(2)}) collective-permute-start(bf16[256,128]{1,0:T(8,128)(2,1)S(1)} %maximum_select_fusion.1), channel_id=1, source_target_pairs={{2,0},{4,2},{6,4},{8,6},{10,8},{12,10},{14,12},{16,14},{18,16},{20... | collective-permute-start | bytes 196616 | tf_op jit(solution)/shard_map/ppermute | solution.py:28
  35.8 1.9 collective-permute-done.3
  37.7 4.4 %collective-permute-start.11 = (bf16[256,128]{1,0:T(8,128)(2,1)S(1)}, bf16[256,128]{1,0:T(8,128)(2,1)S(1)}, u32[]{:S(2)}, u32[]{:S(2)}) collective-permute-start(bf16[256,128]{1,0:T(8,128)(2,1)S(1)} %collective-permute-done.10), channel_id=1, source_target_pairs={{2,0},{4,2},{6,4},{8,6},{10,8},{12,10},{14,12},{16,14},{18,16},{20... | collective-permute-start | bytes 196616 | tf_op jit(solution)/shard_map/ppermute | solution.py:28
  42.2 1.9 collective-permute-done.4
  44.1 4.5 %collective-permute-start.12 = (bf16[256,128]{1,0:T(8,128)(2,1)S(1)}, bf16[256,128]{1,0:T(8,128)(2,1)S(1)}, u32[]{:S(2)}, u32[]{:S(2)}) collective-permute-start(bf16[256,128]{1,0:T(8,128)(2,1)S(1)} %collective-permute-done.11), channel_id=1, source_target_pairs={{2,0},{4,2},{6,4},{8,6},{10,8},{12,10},{14,12},{16,14},{18,16},{20... | collective-permute-start | bytes 196616 | tf_op jit(solution)/shard_map/ppermute | solution.py:28
  48.6 2.0 collective-permute-done.5
  50.6 0.8 multiply_cosine_fusion
  51.4 4.5 %collective-permute-start.13 = (bf16[256,128]{1,0:T(8,128)(2,1)S(1)}, bf16[256,128]{1,0:T(8,128)(2,1)S(1)}, u32[]{:S(2)}, u32[]{:S(2)}) collective-permute-start(bf16[256,128]{1,0:T(8,128)(2,1)S(1)} %collective-permute-done.12), channel_id=1, source_target_pairs={{2,0},{4,2},{6,4},{8,6},{10,8},{12,10},{14,12},{16,14},{18,16},{20... | collective-permute-start | bytes 196616 | tf_op jit(solution)/shard_map/ppermute | solution.py:28
  55.9 1.2 collective-permute-done.6
  57.1 0.6 collective-permute-done.13
  57.8 4.5 %collective-permute-start.14 = (bf16[256,128]{1,0:T(8,128)(2,1)S(1)}, bf16[256,128]{1,0:T(8,128)(2,1)S(1)}, u32[]{:S(2)}, u32[]{:S(2)}) collective-permute-start(bf16[256,128]{1,0:T(8,128)(2,1)S(1)} %collective-permute-done.13), channel_id=1, source_target_pairs={{2,0},{4,2},{6,4},{8,6},{10,8},{12,10},{14,12},{16,14},{18,16},{20... | collective-permute-start | bytes 196616 | tf_op jit(solution)/shard_map/ppermute | solution.py:28
  62.2 1.3 collective-permute-done.7
  63.6 0.6 collective-permute-done.14
  64.2 4.5 %collective-permute-start.15 = (bf16[256,128]{1,0:T(8,128)(2,1)S(1)}, bf16[256,128]{1,0:T(8,128)(2,1)S(1)}, u32[]{:S(2)}, u32[]{:S(2)}) collective-permute-start(bf16[256,128]{1,0:T(8,128)(2,1)S(1)} %collective-permute-done.14), channel_id=1, source_target_pairs={{2,0},{4,2},{6,4},{8,6},{10,8},{12,10},{14,12},{16,14},{18,16},{20... | collective-permute-start | bytes 196616 | tf_op jit(solution)/shard_map/ppermute | solution.py:28
  68.6 1.4 collective-permute-done.8
  70.1 1.6 collective-permute-done.15
  71.6 4.6 %collective-permute-start.16 = (bf16[256,128]{1,0:T(8,128)(2,1)S(1)}, bf16[256,128]{1,0:T(8,128)(2,1)S(1)}, u32[]{:S(2)}, u32[]{:S(2)}) collective-permute-start(bf16[256,128]{1,0:T(8,128)(2,1)S(1)} %collective-permute-done.15), channel_id=1, source_target_pairs={{2,0},{4,2},{6,4},{8,6},{10,8},{12,10},{14,12},{16,14},{18,16},{20... | collective-permute-start | bytes 196616 | tf_op jit(solution)/shard_map/ppermute | solution.py:28
  76.2 1.6 collective-permute-done.9
  78.0 0.1 fusion.25
  78.2 1.2 collective-permute-done.16
  79.5 0.7 gather_fusion
  80.2 0.0 all-gather.7.cloned.1.call-done
  80.2 3.0 %convolution_bitcast_fusion = f32[384,1,128]{0,2,1:T(8,128)S(1)} fusion(bf16[4096,128]{1,0:T(8,128)(2,1)S(1)} %bitcast.92, bf16[384,4096]{1,0:T(8,128)(2,1)} %all-gather.7.cloned.1.call-done), kind=kOutput, calls=%fused_computation.13 | convolution fusion | flops 402653184 | bytes 4390912 | tf_op jit(solution)/shard_map/dot_general | solution.py:104
  83.2 0.5 fusion.20
  83.7 27.4 %all-gather.9.cloned.1.call-done = bf16[4096,512]{1,0:T(8,128)(2,1)} async-done(((bf16[256,512]{1,0:T(8,128)(2,1)}), bf16[4096,512]{1,0:T(8,128)(2,1)}) %all-gather.9.cloned.1.call-update) | async-done | bytes 4194320 | tf_op jit(solution)/shard_map/all_gather | solution.py:99
  111.0 5.5 %fusion.40 = f32[512,384]{1,0:T(8,128)S(1)} fusion(bf16[4096,512]{1,0:T(8,128)(2,1)} %all-gather.9.cloned.1.call-done, bf16[384,4096]{1,0:T(8,128)(2,1)} %all-gather.7.cloned.1.call-done), kind=kOutput, calls=%fused_computation.104 | convolution fusion | flops 1610612736 | bytes 8126464 | tf_op jit(solution)/shard_map/dot_general | solution.py:103
  116.6 0.1 fusion.39
  116.6 0.3 copy.28
  116.9 0.3 copy.27
  117.2 0.2 subtract_convert_fusion
  117.4 0.7 fusion.1
  118.1 0.5 fusion
  118.6 31.0 %all-gather.5.cloned.1.call-done = bf16[4096,128]{1,0:T(8,128)(2,1)} async-done(((bf16[256,128]{1,0:T(8,128)(2,1)}), bf16[4096,128]{1,0:T(8,128)(2,1)}) %all-gather.5.cloned.1.call-update) | async-done | bytes 1048592 | tf_op jit(solution)/shard_map/all_gather | solution.py:101
  149.7 4.1 %convolution_convert_fusion.1 = bf16[128,4,384]{2,0,1:T(8,128)(2,1)S(1)} fusion(f32[384,384,4]{1,0,2:T(8,128)S(1)} %get-tuple-element.16, f32[4,384]{1,0:T(4,128)S(1)} %fusion, f32[4,384]{1,0:T(4,128)S(1)} %get-tuple-element.15, pred[384,384]{0,1:T(8,128)(4,1)S(1)} %iota_compare_fusion, bf16[4096,128]{1,0:T(8,128)(2,1)} %all-gather.5.cloned.1.call-done, ...), kind=kOutput, calls=%fused_computation.7 | convolution fusion | flops 556843008 | bytes 7106560 | tf_op jit(solution)/shard_map/chqk,ckd->cqhd/dot_general | solution.py:125
  153.7 50.1 %all-gather.11.cloned.1.call-done = bf16[512,4096]{1,0:T(8,128)(2,1)} async-done(((bf16[512,256]{1,0:T(8,128)(2,1)}), bf16[512,4096]{1,0:T(8,128)(2,1)}) %all-gather.11.cloned.1.call-update) | async-done | bytes 4194320 | tf_op jit(solution)/shard_map/all_gather | solution.py:91
  203.8 5.7 %convolution_convert_fusion = bf16[384,4096]{1,0:T(8,128)(2,1)} fusion(bf16[384,512]{0,1:T(8,128)(2,1)S(1)} %bitcast.95, bf16[512,4096]{1,0:T(8,128)(2,1)} %all-gather.11.cloned.1.call-done), kind=kOutput, calls=%fused_computation.1 | convolution fusion | flops 1612185600 | bytes 7733248 | tf_op jit(solution)/shard_map/dot_general | solution.py:129
  209.5 0.0 reduce-scatter.2.cloned.1.call-update
  209.5 41.7 %reduce-scatter.2.cloned.1.call-done = bf16[192,4096]{1,0:T(8,128)(2,1)} async-done(((bf16[384,4096]{1,0:T(8,128)(2,1)}), bf16[192,4096]{1,0:T(8,128)(2,1)}) %reduce-scatter.2.cloned.1.call-update) | async-done | bytes 1572880 | tf_op jit(solution)/shard_map/reduce_scatter | solution.py:130
  (45 shorter events, 0.4 us)
Async XLA Ops:
  6.5 11.0 %copy-start = (f32[8,32]{1,0:T(8,128)S(1)}, f32[8,32]{1,0:T(8,128)}, u32[]{:S(2)}) copy-start(f32[8,32]{1,0:T(8,128)} %param.17) | copy-start | bytes 3076
  6.5 4.0 %copy-start.2 = (bf16[256,64]{0,1:T(8,128)(2,1)S(1)}, bf16[256,64]{0,1:T(8,128)(2,1)}, u32[]{:S(2)}) copy-start(bf16[256,64]{0,1:T(8,128)(2,1)} %param.14) | copy-start | bytes 98308
  6.5 4.1 %copy-start.3 = (bf16[256,64]{0,1:T(8,128)(2,1)S(1)}, bf16[256,64]{0,1:T(8,128)(2,1)}, u32[]{:S(2)}) copy-start(bf16[256,64]{0,1:T(8,128)(2,1)} %param.12) | copy-start | bytes 98308
  6.5 4.2 %copy-start.4 = (f32[32,1]{0,1:T(1,128)S(1)}, f32[32,1]{0,1:T(1,128)}, u32[]{:S(2)}) copy-start(f32[32,1]{0,1:T(1,128)} %param.15) | copy-start | bytes 388
  6.5 4.4 %copy-start.5 = (f32[32,1]{0,1:T(1,128)S(1)}, f32[32,1]{0,1:T(1,128)}, u32[]{:S(2)}) copy-start(f32[32,1]{0,1:T(1,128)} %param.13) | copy-start | bytes 388
  6.5 11.3 %copy-start.1 = (bf16[512,256]{1,0:T(8,128)(2,1)S(1)}, bf16[512,256]{1,0:T(8,128)(2,1)}, u32[]{:S(2)}) copy-start(bf16[512,256]{1,0:T(8,128)(2,1)} %param.16) | copy-start | bytes 786436
  6.6 73.7 %all-gather.7.cloned.1.call-start = ((), (), s32[]{:S(2)}) async-start(), calls=%async_computation.2 | async-start | bytes 4718592 | tf_op jit(solution)/shard_map/all_gather | solution.py:92
  7.3 103.7 %all-gather.9.cloned.1.call-start = ((), (), s32[]{:S(2)}) async-start(), calls=%async_computation.3 | async-start | bytes 4456448 | tf_op jit(solution)/shard_map/all_gather | solution.py:99
  10.4 139.2 %all-gather.5.cloned.1.call-start = ((), (), s32[]{:S(2)}) async-start(), calls=%async_computation.1 | async-start | bytes 1114112 | tf_op jit(solution)/shard_map/all_gather | solution.py:101
  11.4 5.2 %collective-permute-start = (bf16[256,64]{1,0:T(8,128)(2,1)S(1)}, bf16[256,64]{1,0:T(8,128)(2,1)S(1)}, u32[]{:S(2)}, u32[]{:S(2)}) collective-permute-start(bf16[256,64]{1,0:T(8,128)(2,1)S(1)} %get-tuple-element.13), channel_id=1, source_target_pairs={{0,1},{1,0},{2,3},{3,2},{4,5},{5,4},{6,7},{7,6},{8,9},{9,8},{10,11... | collective-permute-start | bytes 98312 | tf_op jit(solution)/shard_map/ppermute | solution.py:38
  17.4 186.4 %all-gather.11.cloned.1.call-start = ((), (), s32[]{:S(2)}) async-start(), calls=%async_computation.4 | async-start | bytes 4456448 | tf_op jit(solution)/shard_map/all_gather | solution.py:91
  19.1 232.1 %reduce-scatter.2.cloned.1.call-start = ((), (), s32[]{:S(2)}) async-start(), calls=%async_computation.5 | async-start | bytes 4718592 | tf_op jit(solution)/shard_map/reduce_scatter | solution.py:130
  19.1 5.7 %collective-permute-start.1 = (bf16[256,64]{1,0:T(8,128)(2,1)S(1)}, bf16[256,64]{1,0:T(8,128)(2,1)S(1)}, u32[]{:S(2)}, u32[]{:S(2)}) collective-permute-start(bf16[256,64]{1,0:T(8,128)(2,1)S(1)} %get-tuple-element.14), channel_id=1, source_target_pairs={{0,1},{1,0},{2,3},{3,2},{4,5},{5,4},{6,7},{7,6},{8,9},{9,8},{10,11... | collective-permute-start | bytes 98312 | tf_op jit(solution)/shard_map/ppermute | solution.py:38
  24.9 6.4 %collective-permute-start.2 = (bf16[256,128]{1,0:T(8,128)(2,1)S(1)}, bf16[256,128]{1,0:T(8,128)(2,1)S(1)}, u32[]{:S(2)}, u32[]{:S(2)}) collective-permute-start(bf16[256,128]{1,0:T(8,128)(2,1)S(1)} %maximum_select_fusion.1), channel_id=1, source_target_pairs={{0,2},{2,4},{4,6},{6,8},{8,10},{10,12},{12,14},{14,16},{16,18},{18... | collective-permute-start | bytes 196616 | tf_op jit(solution)/shard_map/ppermute | solution.py:26
  31.3 6.4 %collective-permute-start.3 = (bf16[256,128]{1,0:T(8,128)(2,1)S(1)}, bf16[256,128]{1,0:T(8,128)(2,1)S(1)}, u32[]{:S(2)}, u32[]{:S(2)}) collective-permute-start(bf16[256,128]{1,0:T(8,128)(2,1)S(1)} %collective-permute-done.2), channel_id=1, source_target_pairs={{0,2},{2,4},{4,6},{6,8},{8,10},{10,12},{12,14},{14,16},{16,18},{18... | collective-permute-start | bytes 196616 | tf_op jit(solution)/shard_map/ppermute | solution.py:26
  31.3 6.4 %collective-permute-start.10 = (bf16[256,128]{1,0:T(8,128)(2,1)S(1)}, bf16[256,128]{1,0:T(8,128)(2,1)S(1)}, u32[]{:S(2)}, u32[]{:S(2)}) collective-permute-start(bf16[256,128]{1,0:T(8,128)(2,1)S(1)} %maximum_select_fusion.1), channel_id=1, source_target_pairs={{2,0},{4,2},{6,4},{8,6},{10,8},{12,10},{14,12},{16,14},{18,16},{20... | collective-permute-start | bytes 196616 | tf_op jit(solution)/shard_map/ppermute | solution.py:28
  37.7 6.4 %collective-permute-start.4 = (bf16[256,128]{1,0:T(8,128)(2,1)S(1)}, bf16[256,128]{1,0:T(8,128)(2,1)S(1)}, u32[]{:S(2)}, u32[]{:S(2)}) collective-permute-start(bf16[256,128]{1,0:T(8,128)(2,1)S(1)} %collective-permute-done.3), channel_id=1, source_target_pairs={{0,2},{2,4},{4,6},{6,8},{8,10},{10,12},{12,14},{14,16},{16,18},{18... | collective-permute-start | bytes 196616 | tf_op jit(solution)/shard_map/ppermute | solution.py:26
  37.7 6.4 %collective-permute-start.11 = (bf16[256,128]{1,0:T(8,128)(2,1)S(1)}, bf16[256,128]{1,0:T(8,128)(2,1)S(1)}, u32[]{:S(2)}, u32[]{:S(2)}) collective-permute-start(bf16[256,128]{1,0:T(8,128)(2,1)S(1)} %collective-permute-done.10), channel_id=1, source_target_pairs={{2,0},{4,2},{6,4},{8,6},{10,8},{12,10},{14,12},{16,14},{18,16},{20... | collective-permute-start | bytes 196616 | tf_op jit(solution)/shard_map/ppermute | solution.py:28
  44.1 6.5 %collective-permute-start.5 = (bf16[256,128]{1,0:T(8,128)(2,1)S(1)}, bf16[256,128]{1,0:T(8,128)(2,1)S(1)}, u32[]{:S(2)}, u32[]{:S(2)}) collective-permute-start(bf16[256,128]{1,0:T(8,128)(2,1)S(1)} %collective-permute-done.4), channel_id=1, source_target_pairs={{0,2},{2,4},{4,6},{6,8},{8,10},{10,12},{12,14},{14,16},{16,18},{18... | collective-permute-start | bytes 196616 | tf_op jit(solution)/shard_map/ppermute | solution.py:26
  44.1 7.2 %collective-permute-start.12 = (bf16[256,128]{1,0:T(8,128)(2,1)S(1)}, bf16[256,128]{1,0:T(8,128)(2,1)S(1)}, u32[]{:S(2)}, u32[]{:S(2)}) collective-permute-start(bf16[256,128]{1,0:T(8,128)(2,1)S(1)} %collective-permute-done.11), channel_id=1, source_target_pairs={{2,0},{4,2},{6,4},{8,6},{10,8},{12,10},{14,12},{16,14},{18,16},{20... | collective-permute-start | bytes 196616 | tf_op jit(solution)/shard_map/ppermute | solution.py:28
  50.6 6.5 %collective-permute-start.6 = (bf16[256,128]{1,0:T(8,128)(2,1)S(1)}, bf16[256,128]{1,0:T(8,128)(2,1)S(1)}, u32[]{:S(2)}, u32[]{:S(2)}) collective-permute-start(bf16[256,128]{1,0:T(8,128)(2,1)S(1)} %collective-permute-done.5), channel_id=1, source_target_pairs={{0,2},{2,4},{4,6},{6,8},{8,10},{10,12},{12,14},{14,16},{16,18},{18... | collective-permute-start | bytes 196616 | tf_op jit(solution)/shard_map/ppermute | solution.py:26
  51.4 6.4 %collective-permute-start.13 = (bf16[256,128]{1,0:T(8,128)(2,1)S(1)}, bf16[256,128]{1,0:T(8,128)(2,1)S(1)}, u32[]{:S(2)}, u32[]{:S(2)}) collective-permute-start(bf16[256,128]{1,0:T(8,128)(2,1)S(1)} %collective-permute-done.12), channel_id=1, source_target_pairs={{2,0},{4,2},{6,4},{8,6},{10,8},{12,10},{14,12},{16,14},{18,16},{20... | collective-permute-start | bytes 196616 | tf_op jit(solution)/shard_map/ppermute | solution.py:28
  57.1 6.5 %collective-permute-start.7 = (bf16[256,128]{1,0:T(8,128)(2,1)S(1)}, bf16[256,128]{1,0:T(8,128)(2,1)S(1)}, u32[]{:S(2)}, u32[]{:S(2)}) collective-permute-start(bf16[256,128]{1,0:T(8,128)(2,1)S(1)} %collective-permute-done.6), channel_id=1, source_target_pairs={{0,2},{2,4},{4,6},{6,8},{8,10},{10,12},{12,14},{14,16},{16,18},{18... | collective-permute-start | bytes 196616 | tf_op jit(solution)/shard_map/ppermute | solution.py:26
  57.8 6.4 %collective-permute-start.14 = (bf16[256,128]{1,0:T(8,128)(2,1)S(1)}, bf16[256,128]{1,0:T(8,128)(2,1)S(1)}, u32[]{:S(2)}, u32[]{:S(2)}) collective-permute-start(bf16[256,128]{1,0:T(8,128)(2,1)S(1)} %collective-permute-done.13), channel_id=1, source_target_pairs={{2,0},{4,2},{6,4},{8,6},{10,8},{12,10},{14,12},{16,14},{18,16},{20... | collective-permute-start | bytes 196616 | tf_op jit(solution)/shard_map/ppermute | solution.py:28
  63.6 6.5 %collective-permute-start.8 = (bf16[256,128]{1,0:T(8,128)(2,1)S(1)}, bf16[256,128]{1,0:T(8,128)(2,1)S(1)}, u32[]{:S(2)}, u32[]{:S(2)}) collective-permute-start(bf16[256,128]{1,0:T(8,128)(2,1)S(1)} %collective-permute-done.7), channel_id=1, source_target_pairs={{0,2},{2,4},{4,6},{6,8},{8,10},{10,12},{12,14},{14,16},{16,18},{18... | collective-permute-start | bytes 196616 | tf_op jit(solution)/shard_map/ppermute | solution.py:26
  64.2 7.5 %collective-permute-start.15 = (bf16[256,128]{1,0:T(8,128)(2,1)S(1)}, bf16[256,128]{1,0:T(8,128)(2,1)S(1)}, u32[]{:S(2)}, u32[]{:S(2)}) collective-permute-start(bf16[256,128]{1,0:T(8,128)(2,1)S(1)} %collective-permute-done.14), channel_id=1, source_target_pairs={{2,0},{4,2},{6,4},{8,6},{10,8},{12,10},{14,12},{16,14},{18,16},{20... | collective-permute-start | bytes 196616 | tf_op jit(solution)/shard_map/ppermute | solution.py:28
  70.1 7.8 %collective-permute-start.9 = (bf16[256,128]{1,0:T(8,128)(2,1)S(1)}, bf16[256,128]{1,0:T(8,128)(2,1)S(1)}, u32[]{:S(2)}, u32[]{:S(2)}) collective-permute-start(bf16[256,128]{1,0:T(8,128)(2,1)S(1)} %collective-permute-done.8), channel_id=1, source_target_pairs={{0,2},{2,4},{4,6},{6,8},{8,10},{10,12},{12,14},{14,16},{16,18},{18... | collective-permute-start | bytes 196616 | tf_op jit(solution)/shard_map/ppermute | solution.py:26
  71.6 7.8 %collective-permute-start.16 = (bf16[256,128]{1,0:T(8,128)(2,1)S(1)}, bf16[256,128]{1,0:T(8,128)(2,1)S(1)}, u32[]{:S(2)}, u32[]{:S(2)}) collective-permute-start(bf16[256,128]{1,0:T(8,128)(2,1)S(1)} %collective-permute-done.15), channel_id=1, source_target_pairs={{2,0},{4,2},{6,4},{8,6},{10,8},{12,10},{14,12},{16,14},{18,16},{20... | collective-permute-start | bytes 196616 | tf_op jit(solution)/shard_map/ppermute | solution.py:28
Sparse Core Ops, SparseCore 0:
  8.9 48.3 all-gather.6
  59.5 51.4 all-gather.8
  113.2 36.4 all-gather.4
  151.7 52.1 all-gather.10
  209.7 41.4 reduce-scatter.1
